TPU v7x, 32 devices: a whole 2x2x4 slice. The times are simulated.
32 devices in a mesh: section: 2 (over x), dp: 16 (over z, y, core).
Axes of the slice: x: 2, y: 2, z: 4, core: 2. Of those that a mesh axis runs over, the one named last changes fastest.
Arguments:
- block_ends: bfloat16 [2, 2, 16384, 1024], P('section', None, 'dp'), may hold values from -6 to 6
- proj_in: bfloat16 [2, 524288], P('section', 'dp'), may hold values from -0.1875 to 0.1875
- proj_out: bfloat16 [2, 524288], P('section', 'dp'), may hold values from -0.25 to 0.25
- conv_taps: bfloat16 [2, 4, 262144], P('section', None, 'dp'), may hold values from -0.125 to 0.125
- norm_gains: float32 [2, 2048], P('section'), may hold values from 0.1 to 1.9
- bias_terms: float32 [2, 3072], P('section'), may hold values from -2 to 2
- lengths: int32 [2, 16, 8], P(None, 'dp'), may hold values from 1 to 512, 1024 in all within a row
- dilation: int32 [2], replicated, may hold values from 1 to 64, as said below
Outputs:
- activations: bfloat16 [2, 2, 16384, 1024], P('section', None, 'dp')
- grads_io: float32 [2, 2, 16384, 1024], P('section', None, 'dp')
- grad_proj_in: float32 [2, 524288], P('section', 'dp')
- grad_proj_out: float32 [2, 524288], P('section', 'dp')
- grad_conv_taps: float32 [2, 4, 262144], P('section', None, 'dp')
- grad_norm_gains: float32 [2, 2048], P('section')
- grad_bias_terms: float32 [2, 3072], P('section')
Inputs may be any that keep to these rules, and one draw needn't show every extreme that they name: Each sequence's 8 sentence lengths add up to 1024. `dilation`: the two dilations differ.
All inputs are finite; a program needn't handle non-finite values.
Results may differ from a plain program's by a relative error of at most 0.0096.
Values may be sent and summed in bfloat16 or wider, within the bound.
A program may use at most 256 MiB of HBM per device.

v0:
```python
import jax
import jax.numpy as jnp
from jax import lax
from jax.sharding import PartitionSpec as P

D = 1024
H = 512
LEN = 1024


epsilon = 1e-05


def shifted(value, axis, steps):
    count = lax.axis_size(axis)
    initial, last = (max(0, -steps), min(count, count - steps))
    return lax.ppermute(value, axis, [(source, source + steps) for source in range(initial, last)])


def norm_gelu(values, gain, shift_bias):
    centre = values - jnp.mean(values, axis=-1, keepdims=True)
    spread = jnp.mean(centre * centre, axis=-1, keepdims=True)
    return jax.nn.gelu(centre * lax.rsqrt(spread + epsilon) * gain + shift_bias)


def product(left, right):
    return jnp.dot(left, right, preferred_element_type=jnp.float32)


def contract_rows(left, right):
    return lax.dot_general(
        left, right, (((0,), (0,)), ((), ())), preferred_element_type=jnp.float32
    )


def contract_columns(left, right):
    return lax.dot_general(
        left, right, (((1,), (1,)), ((), ())), preferred_element_type=jnp.float32
    )


def tap_masks(sentence_lengths, offsets, seq_len):
    bounds = jnp.cumsum(sentence_lengths, axis=-1)
    position = jnp.arange(seq_len, dtype=jnp.int32)
    sentence = jnp.sum((position[None, :, None] >= bounds[:, None, :]).astype(jnp.int32), axis=-1)
    result = []
    for offset in offsets:
        source = position + offset
        inside = (source >= 0) & (source < seq_len)
        partner = jnp.roll(sentence, -offset, axis=1)
        result.append((inside[None, :] & (partner == sentence)).astype(jnp.bfloat16))
    return result


def tap_rows(values, masks, offsets, seq_len):
    shaped = values.reshape(-1, seq_len, values.shape[-1])
    pieces = [
        jnp.roll(shaped, -offset, axis=1) * tap_mask[:, :, None]
        for offset, tap_mask in zip(offsets, masks)
    ]
    return jnp.concatenate(pieces, axis=-1).reshape(values.shape[0], -1)


def untap_rows(grads, masks, offsets, seq_len):
    channels = grads.shape[-1] // len(offsets)
    shaped = grads.reshape(-1, seq_len, len(offsets), channels)
    summed = jnp.zeros(shaped.shape[:2] + (channels,), jnp.float32)
    for tap_index, offset in enumerate(offsets):
        weighted = shaped[:, :, tap_index] * masks[tap_index][:, :, None].astype(jnp.float32)
        summed = summed + jnp.roll(weighted, offset, axis=1)
    return summed.reshape(grads.shape[0], channels)


def split_params(gains, biases):
    return (
        (gains[:D], biases[:D]),
        (gains[D : D + H], biases[2 * D : 2 * D + H]),
        (gains[D + H :], biases[2 * D + H :]),
        biases[D : 2 * D],
    )


def block_forward(block_in, weights, masks, offsets, gains, biases, leading, seq_len):
    weight_in, weight_out, kernel_low, kernel_high = weights
    first_norm, second_norm, third_norm, out_bias = split_params(gains, biases)
    in_float = block_in.astype(jnp.float32)
    a_first = norm_gelu(in_float, first_norm[0], first_norm[1]).astype(jnp.bfloat16)
    hidden = product(a_first, weight_in)
    a_second = norm_gelu(hidden, second_norm[0], second_norm[1]).astype(jnp.bfloat16)
    conv_base = product(tap_rows(a_second, masks[:3], offsets[:3], seq_len), kernel_low)

    def high_taps():
        return product(tap_rows(a_second, masks[3:], offsets[3:], seq_len), kernel_high)

    def no_taps():
        return jnp.zeros_like(conv_base)

    conv_out = conv_base + lax.cond(leading, high_taps, no_taps)
    a_third = norm_gelu(conv_out, third_norm[0], third_norm[1]).astype(jnp.bfloat16)
    return (in_float + product(a_third, weight_out) + out_bias).astype(jnp.bfloat16)


def block_backward(block_in, grad_out, weights, masks, offsets, gains, biases, leading, seq_len):
    weight_in, weight_out, kernel_low, kernel_high = weights
    first_norm, second_norm, third_norm, out_bias = split_params(gains, biases)
    in_float = block_in.astype(jnp.float32)
    first_act, first_pull = jax.vjp(norm_gelu, in_float, first_norm[0], first_norm[1])
    a_first = first_act.astype(jnp.bfloat16)
    hidden = product(a_first, weight_in)
    second_act, second_pull = jax.vjp(norm_gelu, hidden, second_norm[0], second_norm[1])
    a_second = second_act.astype(jnp.bfloat16)
    low_rows = tap_rows(a_second, masks[:3], offsets[:3], seq_len)
    conv_base = product(low_rows, kernel_low)

    def high_taps():
        return product(tap_rows(a_second, masks[3:], offsets[3:], seq_len), kernel_high)

    def no_taps():
        return jnp.zeros_like(conv_base)

    conv_out = conv_base + lax.cond(leading, high_taps, no_taps)
    third_act, third_pull = jax.vjp(norm_gelu, conv_out, third_norm[0], third_norm[1])
    a_third = third_act.astype(jnp.bfloat16)
    grad_weight_out = contract_rows(a_third, grad_out)
    grad_out_bias = jnp.sum(grad_out.astype(jnp.float32), axis=0)
    grad_conv, grad_gain_three, grad_bias_three = third_pull(contract_columns(grad_out, weight_out))
    grad_conv = grad_conv.astype(jnp.bfloat16)
    grad_kernel_low = contract_rows(low_rows, grad_conv)

    def high_backward():
        high_rows = tap_rows(a_second, masks[3:], offsets[3:], seq_len)
        back_rows = untap_rows(
            contract_columns(grad_conv, kernel_high), masks[3:], offsets[3:], seq_len
        )
        return (contract_rows(high_rows, grad_conv), back_rows)

    def high_skip():
        return (jnp.zeros(kernel_high.shape, jnp.float32), jnp.zeros(hidden.shape, jnp.float32))

    grad_kernel_high, grad_high_rows = lax.cond(leading, high_backward, high_skip)
    grad_a_second = untap_rows(
        contract_columns(grad_conv, kernel_low), masks[:3], offsets[:3], seq_len
    )
    grad_hidden, grad_gain_two, grad_bias_two = second_pull(grad_a_second + grad_high_rows)
    grad_hidden = grad_hidden.astype(jnp.bfloat16)
    grad_weight_in = contract_rows(a_first, grad_hidden)
    grad_branch, grad_gain_one, grad_bias_one = first_pull(contract_columns(grad_hidden, weight_in))
    grad_in = grad_out.astype(jnp.float32) + grad_branch
    gain_grads = jnp.concatenate([grad_gain_one, grad_gain_two, grad_gain_three])
    bias_grads = jnp.concatenate([grad_bias_one, grad_out_bias, grad_bias_two, grad_bias_three])
    return (
        grad_in,
        (
            grad_weight_in,
            grad_weight_out,
            grad_kernel_low,
            grad_kernel_high,
            gain_grads,
            bias_grads,
        ),
    )


def local(block_ends, proj_in, proj_out, conv_taps, norm_gains, bias_terms, lengths, dilation):
    seq_len = LEN
    leading = lax.axis_index("section") == 0
    spacing = jnp.where(leading, dilation[0], dilation[1])
    offsets = [(tap_index - 2) * spacing for tap_index in range(5)]
    gains = norm_gains[0]
    biases = bias_terms[0]
    micro = block_ends.shape[1]
    row_count = block_ends.shape[2]
    local_ends = block_ends[0]

    def fetch():
        weight_in, weight_out, own_taps = (
            lax.all_gather(proj_in, "dp", axis=1, tiled=True),
            lax.all_gather(proj_out, "dp", axis=1, tiled=True),
            lax.all_gather(conv_taps[0], "dp", axis=1, tiled=True),
        )
        extra_tap = shifted(own_taps[0:1], "section", -1)
        kernel_low = jnp.where(leading, own_taps[0:3], own_taps[1:4]).reshape(3 * H, H)
        kernel_high = jnp.concatenate([own_taps[3:4], extra_tap], axis=0).reshape(2 * H, H)
        return (weight_in.reshape(D, H), weight_out.reshape(H, D), kernel_low, kernel_high)

    def masks_for(lead_batch, follow_batch):
        chosen = jnp.where(leading, lengths[lead_batch], lengths[follow_batch])
        return tap_masks(chosen, offsets, seq_len)

    weights = fetch()
    blank = jnp.zeros((row_count, D), jnp.bfloat16)
    arriving = blank
    outputs_forward = []
    kept_inputs = []
    for moment in range(micro + 1):
        own_input = local_ends[moment] if moment < micro else blank
        block_in = jnp.where(leading, own_input, arriving)
        if moment >= 1:
            kept_inputs.append(arriving)
        masks = masks_for(min(moment, micro - 1), max(moment - 1, 0))
        result = block_forward(block_in, weights, masks, offsets, gains, biases, leading, seq_len)
        outputs_forward.append(result)
        if moment < micro:
            arriving = shifted(result, "section", 1)
    activations = jnp.stack(
        [
            jnp.where(leading, outputs_forward[batch], outputs_forward[batch + 1])
            for batch in range(micro)
        ]
    )[None]
    weights = fetch()
    arriving = blank
    grads_in = []
    summed = None
    for moment in range(micro + 1):
        follow_input = kept_inputs[moment] if moment < micro else blank
        lead_input = local_ends[moment - 1] if moment >= 1 else blank
        block_in = jnp.where(leading, lead_input, follow_input)
        follow_grad = local_ends[moment] if moment < micro else blank
        grad_out = jnp.where(leading, arriving, follow_grad)
        masks = masks_for(max(moment - 1, 0), min(moment, micro - 1))
        grad_in, terms = block_backward(
            block_in, grad_out, weights, masks, offsets, gains, biases, leading, seq_len
        )
        grads_in.append(grad_in)
        summed = terms if summed is None else jax.tree.map(jnp.add, summed, terms)
        if moment < micro:
            arriving = shifted(grad_in.astype(jnp.bfloat16), "section", -1)
    grads_io = jnp.stack(
        [jnp.where(leading, grads_in[batch + 1], grads_in[batch]) for batch in range(micro)]
    )[None]
    grad_weight_in, grad_weight_out, grad_kernel_low, grad_kernel_high, gain_grads, bias_grads = (
        summed
    )
    low_flat = grad_kernel_low.reshape(3, H * H)
    high_flat = grad_kernel_high.reshape(2, H * H)
    passed = shifted(high_flat[1:2].astype(jnp.bfloat16), "section", 1).astype(jnp.float32)
    own_grads = jnp.where(
        leading,
        jnp.concatenate([low_flat, high_flat[0:1]], axis=0),
        jnp.concatenate([passed, low_flat], axis=0),
    )
    part_in, part_out, part_taps = (
        lax.psum_scatter(grad_weight_in.reshape(1, D * H), "dp", scatter_dimension=1, tiled=True),
        lax.psum_scatter(grad_weight_out.reshape(1, H * D), "dp", scatter_dimension=1, tiled=True),
        lax.psum_scatter(own_grads, "dp", scatter_dimension=1, tiled=True),
    )
    gain_sum, bias_sum = lax.psum((gain_grads[None], bias_grads[None]), "dp")
    return (activations, grads_io, part_in, part_out, part_taps[None], gain_sum, bias_sum)


def solution(mesh):
    placed = (
        P("section", None, "dp", None),
        P("section", "dp"),
        P("section", "dp"),
        P("section", None, "dp"),
        P("section", None),
        P("section", None),
        P(None, "dp", None),
        P(),
    )
    return jax.shard_map(
        local,
        mesh=mesh,
        in_specs=placed,
        out_specs=(
            P("section", None, "dp", None),
            P("section", None, "dp", None),
            P("section", "dp"),
            P("section", "dp"),
            P("section", None, "dp"),
            P("section", None),
            P("section", None),
        ),
        check_vma=False,
    )
```

profile of v0, /device:TPU:0, one launch (start us, length us, event | category | flops | bytes accessed | tf_op | source)
XLA Modules:
  0.0 801.2 jit_solution(7149553842702065911)
XLA Ops:
  21.2 33.1 %all-gather.5.cloned.1.call-done = bf16[1,524288]{1,0:T(2,128)(2,1)} async-done(((bf16[1,32768]{1,0:T(2,128)(2,1)}), bf16[1,524288]{1,0:T(2,128)(2,1)}) %all-gather.5.cloned.1.call-update) | async-done | bytes 1048592 | tf_op jit(solution)/shard_map/all_gather | solution.py:177
  54.3 22.8 %reduce.22 = bf16[524288]{0:T(1024)(128)(2,1)S(1)} reduce(bf16[1,524288]{1,0:T(2,128)(2,1)} %all-gather.5.cloned.1.call-done, bf16[]{:T(256)} %constant.274), dimensions={0}, to_apply=%all_gather.12.reduce_sub_computation | reduce | bytes 2097154 | tf_op jit(solution)/shard_map/all_gather | solution.py:177
  77.8 18.9 %all-gather.7.cloned.1.call-done = bf16[1,524288]{1,0:T(2,128)(2,1)} async-done(((bf16[1,32768]{1,0:T(2,128)(2,1)}), bf16[1,524288]{1,0:T(2,128)(2,1)}) %all-gather.7.cloned.1.call-update) | async-done | bytes 1048592 | tf_op jit(solution)/shard_map/all_gather | solution.py:178
  96.7 23.0 %reduce.26 = bf16[524288]{0:T(1024)(128)(2,1)S(1)} reduce(bf16[1,524288]{1,0:T(2,128)(2,1)} %all-gather.7.cloned.1.call-done, bf16[]{:T(256)} %constant.274), dimensions={0}, to_apply=%all_gather.14.reduce_sub_computation | reduce | bytes 2097154 | tf_op jit(solution)/shard_map/all_gather | solution.py:178
  131.3 7.8 all-gather.9.cloned.1.call-done
  150.7 20.9 %collective-permute-done = bf16[1,262144]{1,0:T(2,128)(2,1)} collective-permute-done((bf16[1,262144]{1,0:T(2,128)(2,1)}, bf16[1,262144]{1,0:T(2,128)(2,1)}, u32[]{:S(2)}, u32[]{:S(2)}) %collective-permute-start) | collective-permute-done | bytes 524320 | tf_op jit(solution)/shard_map/ppermute | solution.py:17
  179.0 5.9 conditional.9
  205.1 35.4 %collective-permute-done.1 = bf16[1024,1024]{1,0:T(8,128)(2,1)S(1)} collective-permute-done((bf16[1024,1024]{1,0:T(8,128)(2,1)}, bf16[1024,1024]{1,0:T(8,128)(2,1)S(1)}, u32[]{:S(2)}, u32[]{:S(2)}) %collective-permute-start.1) | collective-permute-done | bytes 2097184 | tf_op jit(solution)/shard_map/ppermute | solution.py:17
  253.0 7.4 conditional.12
  274.1 5.7 convolution_bitcast_fusion.2
  279.9 15.8 %conditional.13 = (f32[1024,512]{1,0:T(8,128)}, f32[1024,512]{0,1:T(8,128)}) conditional(s32[]{:T(128)} %convert_element_type.375, () %tuple.82, (bf16[1024,512]{0,1:T(8,128)(2,1)S(1)}, s32[]{:T(128)}, bf16[1,1024]{1,0:T(2,128)(2,1)S(1)}, s32[]{:T(128)}, bf16[1,1024]{1,0:T(2,128)(2,1)S(1)}, /*index=5*/bf16[1024,512]{0,1:T(8,128)(2,1)}, ...), branch_computations={%region_40.47_spmd, %region_41.48_spmd} | conditional | flops 2160592896 | bytes 35685012 | solution.py:140
  299.0 6.4 multiply_reduce_fusion.5
  306.6 6.3 fusion.141
  322.8 6.0 conditional.10
  344.0 7.4 conditional.16
  362.9 22.4 %collective-permute-done.2 = bf16[1024,1024]{1,0:T(8,128)(2,1)S(1)} collective-permute-done((bf16[1024,1024]{1,0:T(8,128)(2,1)}, bf16[1024,1024]{1,0:T(8,128)(2,1)S(1)}, u32[]{:S(2)}, u32[]{:S(2)}) %collective-permute-start.2) | collective-permute-done | bytes 2097184 | tf_op jit(solution)/shard_map/ppermute | solution.py:17
  391.1 6.5 convert_reduce_fusion.6
  413.4 7.3 conditional.14
  439.3 5.2 fusion.381
  449.6 8.5 %conditional.11 = (f32[1024,512]{0,1:T(8,128)}) conditional(s32[]{:T(128)} %convert_element_type.375, () %tuple.78, (bf16[1024,512]{0,1:T(8,128)(2,1)}, s32[]{:T(128)}, bf16[1,1024]{1,0:T(2,128)(2,1)S(1)}, s32[]{:T(128)}, bf16[1,1024]{1,0:T(2,128)(2,1)S(1)}, /*index=5*/bf16[1024,512]{1,0:T(8,128)(2,1)}) %tuple.79), branch_computations={%region_26.31_spmd, %region_27.32_spmd} | conditional | flops 1084227584 | bytes 14692710 | solution.py:98
  464.3 13.0 %conditional.15 = (f32[1024,512]{1,0:T(8,128)}, f32[1024,512]{0,1:T(8,128)}) conditional(s32[]{:T(128)} %convert_element_type.375, () %tuple.86, (bf16[1024,512]{0,1:T(8,128)(2,1)S(1)}, s32[]{:T(128)}, bf16[1,1024]{1,0:T(2,128)(2,1)S(1)}, s32[]{:T(128)}, bf16[1,1024]{1,0:T(2,128)(2,1)S(1)}, /*index=5*/bf16[1024,512]{0,1:T(8,128)(2,1)}, ...), branch_computations={%region_58.65_spmd, %region_59.66_spmd} | conditional | flops 2160592896 | bytes 39879344 | solution.py:140
  480.6 5.8 multiply_reduce_fusion.3
  487.7 5.7 fusion.131
  517.1 27.8 %collective-permute-done.4 = bf16[1024,1024]{1,0:T(8,128)(2,1)S(1)} collective-permute-done((bf16[1024,1024]{1,0:T(8,128)(2,1)S(1)}, bf16[1024,1024]{1,0:T(8,128)(2,1)S(1)}, u32[]{:S(2)}, u32[]{:S(2)}) %collective-permute-start.4) | collective-permute-done | bytes 2097184 | tf_op jit(solution)/shard_map/ppermute | solution.py:17
  550.4 13.3 %conditional.17 = (f32[1024,512]{1,0:T(8,128)}, f32[1024,512]{0,1:T(8,128)}) conditional(s32[]{:T(128)} %convert_element_type.375, () %tuple.90, (bf16[1024,512]{0,1:T(8,128)(2,1)S(1)}, s32[]{:T(128)}, bf16[1,1024]{1,0:T(2,128)(2,1)S(1)}, s32[]{:T(128)}, bf16[1,1024]{1,0:T(2,128)(2,1)S(1)}, /*index=5*/bf16[1024,512]{0,1:T(8,128)(2,1)}, ...), branch_computations={%region_74.81_spmd, %region_75.82_spmd} | conditional | flops 2160592896 | bytes 39879344 | solution.py:140
  583.0 6.2 reshape.1953
  595.9 5.8 multiply_reduce_fusion.1
  619.3 8.9 %fusion.559 = (f32[1024]{0:T(1024)S(1)}, f32[1024]{0:T(1024)S(1)}, f32[1024]{0:T(1024)S(1)}, f32[1024,1024]{1,0:T(8,128)S(1)}) fusion(f32[1024]{0:T(1024)S(1)} %bitcast.454, f32[1024]{0:T(1024)S(1)} %copy-done.99, bf16[1,2,1024,1024]{3,2,1,0:T(8,128)(2,1)} %param.38, pred[]{:T(512)S(6)} %eq.80, f32[1024]{0:T(1024)S(1)} %bitcast.496, ...), kind=kOutput, calls=%fused_computation.925 | convolution fusion | flops 1108341760 | bytes 11567105 | tf_op jit(solution)/shard_map/dot_general | solution.py:37
  631.3 5.6 select_bitcast_fusion
  637.0 60.5 %all-reduce.3 = (f32[1,2048]{1,0:T(1,128)}, f32[1,3072]{1,0:T(1,128)}) all-reduce(f32[1,2048]{1,0:T(1,128)S(1)} %fusion.454, f32[1,3072]{1,0:T(1,128)S(1)} %fusion.453), channel_id=1, replica_groups=mesh['section'=2,'dp'=16] {'dp'}, use_global_device_ids=true, to_apply=%region_92.99 | all-reduce | flops 5120 | bytes 40960 | tf_op jit(solution)/shard_map/psum | solution.py:248
  697.5 8.6 %maximum_bitcast_fusion.18 = f32[1,2,1024,1024]{3,2,1,0:T(8,128)} fusion(f32[1,1024,1024]{2,1,0:T(8,128)} %get-tuple-element.515, f32[1,1024,1024]{2,1,0:T(8,128)} %get-tuple-element.514), kind=kLoop, calls=%fused_computation.153 | loop fusion | flops 2097152 | bytes 16777216 | tf_op jit(solution)/shard_map/broadcast_in_dim | solution.py:229
  706.1 83.5 %all-reduce.7.cloned.1.call-done = (f32[1,524288]{1,0:T(1,128)}, f32[1,524288]{1,0:T(1,128)}, f32[4,262144]{1,0:T(4,128)}) async-done(((f32[1,524288]{1,0:T(1,128)}, f32[1,524288]{1,0:T(1,128)}, f32[4,262144]{1,0:T(4,128)}), (f32[1,524288]{1,0:T(1,128)}, f32[1,524288]{1,0:T(1,128)}, f32[4,262144]{1,0:T(4,128)})) %all-reduce.7.cloned.1.call-update) | async-done | bytes 8388624
  (516 shorter events, 347.2 us)
Async XLA Ops:
  7.2 47.1 %all-gather.5.cloned.1.call-start = ((), (), s32[]{:S(2)}) async-start(), calls=%async_computation | async-start | bytes 2228224 | tf_op jit(solution)/shard_map/all_gather | solution.py:177
  7.9 88.8 %all-gather.7.cloned.1.call-start = ((), (), s32[]{:S(2)}) async-start(), calls=%async_computation.1 | async-start | bytes 2228224 | tf_op jit(solution)/shard_map/all_gather | solution.py:178
  8.6 130.4 %all-gather.9.cloned.1.call-start = ((), (), s32[]{:S(2)}) async-start(), calls=%async_computation.2 | async-start | bytes 2228224 | tf_op jit(solution)/shard_map/all_gather | solution.py:179
  9.4 780.3 %all-reduce.7.cloned.1.call-start = ((), (), s32[]{:S(2)}) async-start(), calls=%async_computation.3 | async-start | bytes 16777216
  18.9 181.2 %copy-start.98 = (f32[1024]{0:T(1024)}, f32[1024]{0:T(1024)S(1)}, u32[]{:S(2)}) copy-start(f32[1024]{0:T(1024)S(1)} %get-tuple-element.596) | copy-start | bytes 12292
  21.1 178.9 %copy-start.104 = (f32[1024]{0:T(1024)}, f32[1024]{0:T(1024)S(1)}, u32[]{:S(2)}) copy-start(f32[1024]{0:T(1024)S(1)} %get-tuple-element.432) | copy-start | bytes 12292
  77.8 43.2 %copy-start.70 = (bf16[1024,512]{1,0:T(8,128)(2,1)}, bf16[1024,512]{1,0:T(8,128)(2,1)S(1)}, u32[]{:S(2)}) copy-start(bf16[1024,512]{1,0:T(8,128)(2,1)S(1)} %reshape.1932) | copy-start | bytes 3145732
  139.1 6.4 copy-start.25
  144.1 27.5 %collective-permute-start = (bf16[1,262144]{1,0:T(2,128)(2,1)}, bf16[1,262144]{1,0:T(2,128)(2,1)}, u32[]{:S(2)}, u32[]{:S(2)}) collective-permute-start(bf16[1,262144]{1,0:T(2,128)(2,1)} %get-tuple-element.528), channel_id=1, source_target_pairs={{16,0},{17,1},{18,2},{19,3},{20,4},{21,5},{22,6},{23,7},{24,8},{25... | collective-permute-start | bytes 1572872 | tf_op jit(solution)/shard_map/ppermute | solution.py:17
  147.5 28.4 %copy-start.31 = (bf16[1,3,262144]{2,1,0:T(4,128)(2,1)}, bf16[1,3,262144]{2,1,0:T(4,128)(2,1)S(1)}, u32[]{:S(2)}) copy-start(bf16[1,3,262144]{2,1,0:T(4,128)(2,1)S(1)} %slice_select_fusion) | copy-start | bytes 4718596
  190.9 9.3 %copy-start.71 = (bf16[1024,512]{1,0:T(8,128)(2,1)S(1)}, bf16[1024,512]{1,0:T(8,128)(2,1)}, u32[]{:S(2)}) copy-start(bf16[1024,512]{1,0:T(8,128)(2,1)} %copy-done.70) | copy-start | bytes 3145732
  194.2 46.4 %collective-permute-start.1 = (bf16[1024,1024]{1,0:T(8,128)(2,1)}, bf16[1024,1024]{1,0:T(8,128)(2,1)S(1)}, u32[]{:S(2)}, u32[]{:S(2)}) collective-permute-start(bf16[1024,1024]{1,0:T(8,128)(2,1)} %fusion.182), channel_id=1, source_target_pairs={{0,16},{1,17},{2,18},{3,19},{4,20},{5,21},{6,22},{7,23},{8,24},{9,... | collective-permute-start | bytes 6291464 | tf_op jit(solution)/shard_map/ppermute | solution.py:17
  204.8 41.2 %copy-start.11 = (f32[1024,512]{0,1:T(8,128)}, f32[1024,512]{0,1:T(8,128)S(1)}, u32[]{:S(2)}) copy-start(f32[1024,512]{0,1:T(8,128)S(1)} %get-tuple-element.574) | copy-start | bytes 6291460
  204.8 41.2 %copy-start.94 = (f32[1024]{0:T(1024)}, f32[1024]{0:T(1024)S(1)}, u32[]{:S(2)}) copy-start(f32[1024]{0:T(1024)S(1)} %broadcast_multiply_fusion.7) | copy-start | bytes 12292
  205.1 36.7 %copy-start.102 = (f32[1024]{0:T(1024)}, f32[1024]{0:T(1024)S(1)}, u32[]{:S(2)}) copy-start(f32[1024]{0:T(1024)S(1)} %multiply_reduce_fusion.9) | copy-start | bytes 12292
  205.1 40.9 %copy-start.96 = (f32[1024]{0:T(1024)}, f32[1024]{0:T(1024)S(1)}, u32[]{:S(2)}) copy-start(f32[1024]{0:T(1024)S(1)} %fusion.487) | copy-start | bytes 12292
  265.4 7.0 copy-start.21
  305.9 7.0 copy-start.37
  305.9 7.0 copy-start.113
  336.2 7.8 copy-start.27
  339.5 45.8 %collective-permute-start.2 = (bf16[1024,1024]{1,0:T(8,128)(2,1)}, bf16[1024,1024]{1,0:T(8,128)(2,1)S(1)}, u32[]{:S(2)}, u32[]{:S(2)}) collective-permute-start(bf16[1024,1024]{1,0:T(8,128)(2,1)} %fusion.192), channel_id=1, source_target_pairs={{0,16},{1,17},{2,18},{3,19},{4,20},{5,21},{6,22},{7,23},{8,24},{9,... | collective-permute-start | bytes 6291464 | tf_op jit(solution)/shard_map/ppermute | solution.py:17
  342.5 48.6 %collective-permute-start.3 = (bf16[1024,1024]{1,0:T(8,128)(2,1)}, bf16[1024,1024]{1,0:T(8,128)(2,1)}, u32[]{:S(2)}, u32[]{:S(2)}) collective-permute-start(bf16[1024,1024]{1,0:T(8,128)(2,1)} %get-tuple-element.524), channel_id=1, source_target_pairs={{16,0},{17,1},{18,2},{19,3},{20,4},{21,5},{22,6},{23,7},{24,8},{25... | collective-permute-start | bytes 6291464 | tf_op jit(solution)/shard_map/ppermute | solution.py:17
  391.1 7.2 copy-start.73
  425.7 7.4 copy-start.23
  463.3 14.1 %copy-start.109 = (f32[1024]{0:T(1024)S(1)}, f32[1024]{0:T(1024)}, u32[]{:S(2)}) copy-start(f32[1024]{0:T(1024)} %convert_element_type.414) | copy-start | bytes 12292
  463.3 14.1 %copy-start.110 = (f32[1024]{0:T(1024)S(1)}, f32[1024]{0:T(1024)}, u32[]{:S(2)}) copy-start(f32[1024]{0:T(1024)} %convert_element_type.415) | copy-start | bytes 12292
  497.4 47.6 %collective-permute-start.4 = (bf16[1024,1024]{1,0:T(8,128)(2,1)S(1)}, bf16[1024,1024]{1,0:T(8,128)(2,1)S(1)}, u32[]{:S(2)}, u32[]{:S(2)}) collective-permute-start(bf16[1024,1024]{1,0:T(8,128)(2,1)S(1)} %fusion.557), channel_id=1, source_target_pairs={{16,0},{17,1},{18,2},{19,3},{20,4},{21,5},{22,6},{23,7},{24,8},{25... | collective-permute-start | bytes 6291464 | tf_op jit(solution)/shard_map/ppermute | solution.py:17
  591.3 21.3 %collective-permute-start.5 = (bf16[1,262144]{1,0:T(2,128)(2,1)S(1)}, bf16[1,262144]{1,0:T(2,128)(2,1)S(1)}, u32[]{:S(2)}, u32[]{:S(2)}) collective-permute-start(bf16[1,262144]{1,0:T(2,128)(2,1)S(1)} %bitcast.432), channel_id=1, source_target_pairs={{0,16},{1,17},{2,18},{3,19},{4,20},{5,21},{6,22},{7,23},{8,24},{9,... | collective-permute-start | bytes 1572872 | tf_op jit(solution)/shard_map/ppermute | solution.py:17
  619.3 8.9 %copy-start.105 = (f32[1024]{0:T(1024)S(1)}, f32[1024]{0:T(1024)}, u32[]{:S(2)}) copy-start(f32[1024]{0:T(1024)} %copy-done.104) | copy-start | bytes 12292
  619.3 8.9 %copy-start.6 = (bf16[1,2,1024,1024]{3,2,1,0:T(8,128)(2,1)S(1)}, bf16[1,2,1024,1024]{3,2,1,0:T(8,128)(2,1)}, u32[]{:S(2)}) copy-start(bf16[1,2,1024,1024]{3,2,1,0:T(8,128)(2,1)} %param.38) | copy-start | bytes 12582916
  619.3 11.5 %copy-start.10 = (f32[1024,1024]{1,0:T(8,128)S(1)}, f32[1024,1024]{1,0:T(8,128)}, u32[]{:S(2)}) copy-start(f32[1024,1024]{1,0:T(8,128)} %copy-done.9) | copy-start | bytes 12582916
  619.3 11.5 %copy-start.47 = (bf16[1024,1024]{1,0:T(8,128)(2,1)S(1)}, bf16[1024,1024]{1,0:T(8,128)(2,1)}, u32[]{:S(2)}) copy-start(bf16[1024,1024]{1,0:T(8,128)(2,1)} %copy-done.45) | copy-start | bytes 6291460
  (107 other events, 360.2 us)
Sparse Core Ops, SparseCore 0:
  10.2 44.1 all-gather.4
  56.5 40.1 all-gather.6
  98.8 40.1 all-gather.8
  618.2 171.3 all-reduce.6
where the time goes:
time: 809 us; the launch traced here: 801 us
  waiting for transfers between devices  257 us (32%)
  other arithmetic  224 us (28%)
  matrix products  159 us (20%)
  local copies, waits for them, and re-layouts  69.4 us (9%)
  blocking collectives  60.5 us (7%)
  between operations  18.6 us (2%)
  starting transfers between devices  9.15 us (1%)
    ppermute x6, waiting for transfers between devices, shifted(): lax.ppermute(value, axis, [(source, source + steps) for source in range(i...  112 us
    unnamed x5, waiting for transfers between devices  85.6 us
    psum x1, blocking collectives, local(): gain_sum, bias_sum = lax.psum((gain_grads[None], bias_grads[None]), 'dp')  60.5 us
    dot_general x15, matrix products, product(): return jnp.dot(left, right, preferred_element_type=jnp.float32)  56.2 us
    mul x23, other arithmetic, tap_rows(): jnp.roll(shaped, -offset, axis=1) * tap_mask[:, :, None]  56.1 us
    dot_general x12, matrix products, contract_columns(): lax.dot_general(left, right, (((1,), (1,)), ((), ())), preferred_element_...  50.7 us
    dot_general x12, matrix products, contract_rows(): lax.dot_general(left, right, (((0,), (0,)), ((), ())), preferred_element_...  36.4 us
    unnamed x245, local copies, waits for them, and re-layouts  33.3 us
  transfers between devices with their start and end apart: 10, of which 10 were waited for; matrix products, arithmetic and copies ran while one was open for 20% of the time, Pallas kernels for 0%

commit v1 on v0

v1 whole, which is shorter than its diff:
```python
import functools

import jax
import jax.numpy as jnp
from jax import lax
from jax.experimental import pallas as pl
from jax.experimental.pallas import tpu as pltpu
from jax.sharding import Mesh
from jax.sharding import PartitionSpec as P

D = 1024
H = 512
LEN = 1024
POSITIONS = 16
RING = 8
TILE = 256
TILES = LEN // TILE
PAD = 128
LANES = 128
PANELS = H // LANES
epsilon = 1e-05
linear_term = 0.7978845608028654
cubic_term = linear_term * 0.044715
kappa = cubic_term ** (1.0 / 3.0)
beta = linear_term / kappa
MESH = pl.DeviceIdType.MESH
F32 = jnp.float32
BF16 = jnp.bfloat16

PIECE = 256
EARLY = ((0, 0, 96), (0, 96, 160), (1, 0, 32))
LATE = ((1, 32, 64), (1, 96, 160))
PARTS = EARLY + LATE
GRAD = 288
HALF = GRAD // 2
ACC_ROWS = 2 * D + 5 * H
STAT = 5 * D


def product(left, right):
    return jnp.dot(left, right, preferred_element_type=F32)


def contract_rows(left, right):
    return lax.dot_general(left, right, (((0,), (0,)), ((), ())), preferred_element_type=F32)


def contract_columns(left, right):
    return lax.dot_general(left, right, (((1,), (1,)), ((), ())), preferred_element_type=F32)


def normalise(values):
    mean = jnp.mean(values, axis=-1, keepdims=True)
    centre = values - mean
    scale = lax.rsqrt(jnp.mean(centre * centre, axis=-1, keepdims=True) + epsilon)
    return centre * scale, mean, scale


def gelu(normal, gain, bias):
    half = normal * (0.5 * gain) + 0.5 * bias
    inner = half * (half * half * (8.0 * cubic_term) + 2.0 * linear_term)
    return half + half * jnp.tanh(inner)


def gelu_norm_back(normal, scale, gain, bias, upstream):
    arg = normal * (kappa * gain) + kappa * bias
    square = arg * arg
    bend = jnp.tanh(arg * (square + beta))
    slope = arg * (3.0 * square + beta)
    double_q = upstream * ((1.0 + bend) * (1.0 + (1.0 - bend) * slope))
    weighted = (0.5 * gain) * double_q
    count = 1.0 / normal.shape[-1]
    mean = jnp.sum(weighted, axis=-1, keepdims=True) * count
    along = jnp.sum(weighted * normal, axis=-1, keepdims=True) * count
    return (weighted - mean - normal * along) * scale, double_q * normal, double_q


def fold_rows(values):
    return jnp.sum(values.reshape(values.shape[0] // 8, 8, values.shape[1]), axis=0)


def ring_chip(place):
    place = lax.rem(place + 2 * RING, RING)
    return jnp.where(place < RING // 2, 2 * place, 2 * (RING - place) - 1)


def kernel(group, dilation, lengths, ends, piece, params, *refs):
    (
        act_out,
        gio_out,
        grad_in_out,
        grad_out_out,
        grad_tap_out,
        gain_out,
        bias_out,
        weights,
        own,
        bufs,
        panels,
        a_first,
        a_second,
        a_third,
        stats,
        bounds,
        acc,
        vec,
        gio_stage,
        act_stage,
        vectors,
        sums,
        tap_send,
        tap_land,
        ring_send,
        ring_recv,
        sib_send,
        sib_recv,
        cross_send,
        cross_recv,
        raw_send,
        raw_recv,
        pass_send,
        pass_recv,
        local_sem,
        act_sem,
        gio_sem,
        red_send,
        red_recv,
        vec_send,
        vec_recv,
        tap_sem,
        ready,
    ) = refs
    section = lax.axis_index("section")
    index = lax.axis_index("dp")
    place, lane = index // group, lax.rem(index, group)
    chip, core = place // 2, lax.rem(place, 2)
    ring = jnp.where(lax.rem(chip, 2) == 0, chip // 2, RING - (chip + 1) // 2)

    def device(sec, position):
        return {"section": sec, "dp": position * group + lane}

    def position(ring_place, which_core):
        return 2 * ring_chip(ring_place) + which_core

    peer = device(1 - section, place)
    sibling = device(section, 2 * chip + 1 - core)
    after = device(section, position(ring + 1, core))
    before = device(section, position(ring - 1, core))

    def remote(src, dst, send, recv, target):
        return pltpu.make_async_remote_copy(
            src_ref=src, dst_ref=dst, send_sem=send, recv_sem=recv, device_id=target, device_id_type=MESH
        )

    barrier = pltpu.get_barrier_semaphore()
    for target in (peer, sibling, after, before):
        pl.semaphore_signal(barrier, inc=1, device_id=target, device_id_type=MESH)
    pl.semaphore_wait(barrier, 4)

    def rows_of(part, origin, half=None):
        sec, first, rows = PARTS[part]
        if half is not None:
            first, rows = first + half * (rows // 2), rows // 2
        return pl.ds(pl.multiple_of((sec * POSITIONS + origin) * PIECE + first, 16), rows)

    def ring_copy(part, hop, way):
        step = 1 if way == 0 else -1
        rows = rows_of(part, position(ring - step * (hop - 1), core), way if hop == 4 else None)
        return remote(
            weights.at[rows], weights.at[rows], ring_send.at[way, part, hop - 1], ring_recv.at[way, part, hop - 1],
            after if way == 0 else before,
        )

    def ring_arrival(part, hop, way):
        step = 1 if way == 0 else -1
        rows = rows_of(part, position(ring - step * hop, core), way if hop == 4 else None)
        return remote(
            weights.at[rows], weights.at[rows], ring_send.at[way, part, hop - 1], ring_recv.at[way, part, hop - 1],
            after if way == 0 else before,
        )

    def share_copy(part, ring_place, slot, which_core):
        rows = rows_of(part, position(ring_place, which_core))
        return remote(
            weights.at[rows], weights.at[rows], sib_send.at[part, slot], sib_recv.at[part, slot], sibling
        )

    def start_part(part):
        for way in range(2):
            ring_copy(part, 1, way).start()
        share_copy(part, ring, 0, core).start()

    def advance(part, hop):
        for way in range(2):
            ring_arrival(part, hop, way).wait_recv()
            if hop < 4:
                ring_copy(part, hop + 1, way).start()
                share_copy(part, ring - hop if way == 0 else ring + hop, 2 * hop - 1 + way, core).start()
        if hop == 4:
            share_copy(part, ring + 4, 7, core).start()

    def wait_shared(parts):
        for part in parts:
            share_copy(part, ring, 0, 1 - core).wait_recv()
            for hop in range(1, 4):
                for way in range(2):
                    share_copy(part, ring - hop if way == 0 else ring + hop, 2 * hop - 1 + way, 1 - core).wait_recv()
            share_copy(part, ring + 4, 7, 1 - core).wait_recv()

    def cross_copy(half, sec):
        first, rows = ((0, 96), (96, 160))[half]
        slot = pl.ds(pl.multiple_of((sec * POSITIONS + place) * PIECE + first, 16), rows)
        return remote(piece.at[pl.ds(first, rows)], weights.at[slot], cross_send.at[half], cross_recv.at[half], peer)

    def cross_params(sec):
        return remote(params, vectors.at[sec], cross_send.at[2], cross_recv.at[2], peer)

    def tile_rows(t):
        return pl.ds(pl.multiple_of(t * TILE, TILE), TILE)

    def raw_copy(t):
        return remote(
            ends.at[section, tile_rows(t)], bufs.at[2, tile_rows(t)], raw_send.at[t], raw_recv.at[t], peer
        )

    for half in range(2):
        cross_copy(half, section).start()
    cross_params(section).start()
    for t in range(TILES):
        raw_copy(t).start()
    own_slot = pl.ds(pl.multiple_of((section * POSITIONS + place) * PIECE, PIECE), PIECE)
    keep_piece = pltpu.make_async_copy(piece, weights.at[own_slot], local_sem.at[0])
    keep_params = pltpu.make_async_copy(params, vectors.at[section], local_sem.at[1])
    keep_ends = pltpu.make_async_copy(ends, own, local_sem.at[2])
    keep_piece.start()
    keep_params.start()
    keep_ends.start()
    keep_piece.wait()

    @pl.when(section == 0)
    def _():
        start_part(0)
        start_part(1)

    @pl.when(section == 1)
    def _():
        start_part(2)

    acc[...] = jnp.zeros_like(acc)
    vec[...] = jnp.zeros_like(vec)
    for half in range(2):
        cross_copy(half, 1 - section).wait_recv()

    @pl.when(section == 0)
    def _():
        start_part(2)

    @pl.when(section == 1)
    def _():
        start_part(0)
        start_part(1)

    for hop in range(1, 5):
        for part in range(3):
            advance(part, hop)
        if hop == 3:
            for part in range(3, 5):
                start_part(part)
    wait_shared(range(3))
    keep_params.wait()
    keep_ends.wait()
    cross_params(1 - section).wait_recv()

    def advance_late(hop):
        for part in range(3, 5):
            advance(part, hop)
        if hop == 4:
            wait_shared(range(3, 5))

    def matrix(sec, first, rows):
        starts = [(sec * POSITIONS + pos) * PIECE + first for pos in range(POSITIONS)]
        return jnp.concatenate([weights[start : start + rows, :] for start in starts], axis=0)

    def weight_in(block):
        return matrix(block, 32, 64)

    def weight_out(block, half):
        return matrix(block, 96 + 32 * half, 32)

    def tap(block, k):
        sec, slot = (0, k) if block == 0 and k < 4 else (1, 0) if block == 0 else (1, k + 1)
        return matrix(sec, 0 if slot == 0 else 128 + 32 * slot, 32)

    def gain(block, norm):
        first, size = ((0, D), (D, H), (D + H, H))[norm]
        return vectors[block, :, first : first + size]

    def bias(block, norm):
        first, size = ((0, D), (2 * D, H), (2 * D + H, H))[norm]
        return vectors[block, :, 2 * D + first : 2 * D + first + size]

    def out_bias(block, half):
        first = 3 * D + half * H
        return vectors[block, :, first : first + H]

    def put_panels(which, base, values):
        for j in range(PANELS):
            panels[which, j, pl.ds(PAD + base, TILE), :] = values[:, j * LANES : (j + 1) * LANES]

    def get_panels(which, start):
        return jnp.concatenate([panels[which, j, pl.ds(start, TILE), :] for j in range(PANELS)], axis=1)

    def shifted(which, base, offset):
        values = get_panels(which, PAD + base + offset)
        inside = (bounds[0, pl.ds(base, TILE), :] <= offset) & (bounds[1, pl.ds(base, TILE), :] > offset)
        return jnp.where(jnp.concatenate([inside] * PANELS, axis=1), values, 0.0).astype(BF16)

    def sentence_bounds(m):
        row = lax.broadcasted_iota(jnp.int32, (LEN, LANES), 0)
        first = jnp.zeros((LEN, LANES), jnp.int32)
        last = jnp.full((LEN, LANES), LEN, jnp.int32)
        reached = jnp.int32(0)
        for j in range(8):
            end = reached + lengths[m, j]
            inside = (row >= reached) & (row < end)
            first = jnp.where(inside, reached, first)
            last = jnp.where(inside, end, last)
            reached = end
        bounds[0] = first - row
        bounds[1] = last - row

    taps = (5, 3)

    def add_rows(first, rows, values):
        acc[pl.ds(first, rows), :] += values

    def forward_in(block, source, t, shift_panel, keep_panel, keep_act):
        base = pl.multiple_of(t * TILE, TILE)
        rows = pl.ds(base, TILE)
        normal, mean, scale = normalise(source[rows, :].astype(F32))
        act = gelu(normal, gain(block, 0), bias(block, 0)).astype(BF16)
        if keep_panel is not None:
            stats[block, 0, rows, :] = mean
            stats[block, 1, rows, :] = scale
        if keep_act:
            a_first[rows, :] = act
        normal, _, scale = normalise(product(act, weight_in(block)))
        act = gelu(normal, gain(block, 1), bias(block, 1)).astype(BF16)
        if keep_panel is not None:
            stats[block, 2, rows, :] = scale
            put_panels(keep_panel, base, normal)
        if keep_act:
            a_second[rows, :] = act
        put_panels(shift_panel, base, act.astype(F32))

    def forward_out(block, source, t, shift_panel, keep_panel, keep_act, store):
        base = pl.multiple_of(t * TILE, TILE)
        rows = pl.ds(base, TILE)
        conv = None
        for k in range(taps[block]):
            term = product(shifted(shift_panel, base, (k - 2) * dilation[block]), tap(block, k))
            conv = term if conv is None else conv + term
        normal, _, scale = normalise(conv)
        if keep_panel is not None:
            stats[block, 3, rows, :] = scale
            put_panels(keep_panel, base, normal)
        if store is None:
            return
        act = gelu(normal, gain(block, 2), bias(block, 2)).astype(BF16)
        if keep_act:
            a_third[rows, :] = act
        for half in range(2):
            cols = slice(half * H, (half + 1) * H)
            residual = source[rows, cols].astype(F32) + product(act, weight_out(block, half))
            store(cols, (residual + out_bias(block, half)).astype(BF16))

    def backward_out(block, grad, t, panel, with_grads):
        base = pl.multiple_of(t * TILE, TILE)
        rows = pl.ds(base, TILE)
        upstream = contract_columns(grad[rows, 0:H], weight_out(block, 0))
        upstream = upstream + contract_columns(grad[rows, H:D], weight_out(block, 1))
        back, double_qn, double_q = gelu_norm_back(
            get_panels(panel, PAD + base), stats[block, 3, rows, :], gain(block, 2), bias(block, 2), upstream
        )
        if with_grads:
            vec[0, :, D + H : 2 * D] += fold_rows(double_qn)
            vec[1, :, D + H : 2 * D] += fold_rows(double_q)
            vec[2, :, 0:D] += fold_rows(grad[rows, :].astype(F32))
            act = a_third[rows, :]
            for half in range(2):
                add_rows(D + half * H, H, contract_rows(act, grad[rows, half * H : (half + 1) * H]))
        put_panels(panel, base, back.astype(BF16).astype(F32))

    def backward_in(block, source, grad, t, panel, normal_panel, with_grads, store):
        base = pl.multiple_of(t * TILE, TILE)
        rows = pl.ds(base, TILE)
        upstream = None
        for k in range(taps[block]):
            moved = shifted(panel, base, (2 - k) * dilation[block])
            term = contract_columns(moved, tap(block, k))
            upstream = term if upstream is None else upstream + term
            if with_grads:
                slot = k if block == 0 else k + 1
                add_rows(2 * D + slot * H, H, contract_rows(a_second[rows, :], moved))
        back, double_qn, double_q = gelu_norm_back(
            get_panels(normal_panel, PAD + base), stats[block, 2, rows, :], gain(block, 1), bias(block, 1), upstream
        )
        back = back.astype(BF16)
        if with_grads:
            vec[0, :, D : D + H] += fold_rows(double_qn)
            vec[1, :, D : D + H] += fold_rows(double_q)
            add_rows(0, D, contract_rows(a_first[rows, :], back))
        upstream = contract_columns(back, weight_in(block))
        scale = stats[block, 1, rows, :]
        normal = (source[rows, :].astype(F32) - stats[block, 0, rows, :]) * scale
        back, double_qn, double_q = gelu_norm_back(normal, scale, gain(block, 0), bias(block, 0), upstream)
        if with_grads:
            vec[0, :, 0:D] += fold_rows(double_qn)
            vec[1, :, 0:D] += fold_rows(double_q)
        store(grad[rows, :].astype(F32) + back)

    def act_copy(m, t, staged):
        src = act_stage.at[lax.rem(t, 2)] if staged else bufs.at[0, tile_rows(t)]
        return pltpu.make_async_copy(src, act_out.at[m, tile_rows(t)], act_sem.at[lax.rem(t, 2)])

    def gio_copy(m, t):
        slot = lax.rem(t, 2)
        return pltpu.make_async_copy(gio_stage.at[slot], gio_out.at[m, tile_rows(t)], gio_sem.at[slot])

    def act_pass(t):
        return remote(
            act_out.at[1, tile_rows(t)], bufs.at[1, tile_rows(t)], pass_send.at[t], pass_recv.at[t], peer
        )

    def grad_pass(t):
        return remote(bufs.at[2, tile_rows(t)], bufs.at[1, tile_rows(t)], pass_send.at[t], pass_recv.at[t], peer)

    def settle(copy, t, count):
        @pl.when(t >= 1)
        def _():
            copy(t - 1).wait()

        @pl.when(t == count - 1)
        def _():
            copy(t).wait()

    @pl.when(section == 0)
    def _():
        @pl.loop(0, 2)
        def _(i):
            m = 1 - i
            source = own.at[m]
            sentence_bounds(m)

            @pl.loop(0, TILES + 1)
            def _(t):
                @pl.when(t < TILES)
                def _():
                    forward_in(0, source, t, 4, 0, True)

                @pl.when(t >= 1)
                def _():
                    done = t - 1

                    def store(cols, values):
                        bufs[0, tile_rows(done), cols] = values

                    forward_out(0, source, done, 4, 1, True, store)
                    act_copy(m, done, False).start()
                    settle(lambda s: act_copy(m, s, False), done, TILES)

                for hop in range(1, 5):

                    @pl.when((i == 0) & (t == hop))
                    def _():
                        advance_late(hop)

            @pl.when(i == 0)
            def _():
                for t in range(TILES):
                    act_pass(t).start()

                @pl.loop(0, TILES + 1)
                def _(t):
                    @pl.when(t < TILES)
                    def _():
                        raw_copy(t).wait_recv()
                        forward_in(1, bufs.at[0], t, 4, 2, False)
                        forward_out(1, bufs.at[0], t, 4, 3, False, None)
                        backward_out(1, bufs.at[2], t, 3, False)

                    @pl.when(t >= 1)
                    def _():
                        done = t - 1

                        def store(values):
                            bufs[2, tile_rows(done), :] = values.astype(BF16)

                        backward_in(1, bufs.at[0], bufs.at[2], done, 3, 2, False, store)

            grad = bufs.at[2 - i]

            @pl.loop(0, TILES + 1)
            def _(t):
                @pl.when((t < TILES) & (i == 1))
                def _():
                    grad_pass(t).wait_recv()

                @pl.when(t < TILES)
                def _():
                    backward_out(0, grad, t, 1, True)

                @pl.when(t >= 1)
                def _():
                    done = t - 1

                    def store(values):
                        gio_stage[lax.rem(done, 2)] = values

                    backward_in(0, source, grad, done, 1, 0, True, store)
                    gio_copy(m, done).start()
                    settle(lambda s: gio_copy(m, s), done, TILES)

        for t in range(TILES):
            act_pass(t).wait_send()

    @pl.when(section == 1)
    def _():
        @pl.loop(0, 2)
        def _(i):
            sentence_bounds(i)
            source = bufs.at[i]
            grad = own.at[i]

            @pl.loop(0, TILES + 2)
            def _(t):
                @pl.when((i == 0) & (t < TILES))
                def _():
                    raw_copy(t).wait_recv()
                    forward_in(0, bufs.at[2], t, 0, None, False)

                @pl.when((i == 0) & (t >= 1) & (t <= TILES))
                def _():
                    done = t - 1

                    def store(cols, values):
                        bufs[0, tile_rows(done), cols] = values

                    forward_out(0, bufs.at[2], done, 0, None, False, store)

                @pl.when((i == 0) & (t == 0))
                def _():
                    advance_late(1)

                @pl.when((i == 0) & (t == 1))
                def _():
                    for hop in range(2, 5):
                        advance_late(hop)

                @pl.when((i == 1) & (t >= 1) & (t <= TILES))
                def _():
                    act_pass(t - 1).wait_recv()

                @pl.when((t >= 1) & (t <= TILES))
                def _():
                    done = t - 1

                    def store(cols, values):
                        act_stage[lax.rem(done, 2), :, cols] = values

                    forward_in(1, source, done, 4, 2, True)
                    forward_out(1, source, done, 4, 3, True, store)
                    act_copy(i, done, True).start()
                    settle(lambda s: act_copy(i, s, True), done, TILES)
                    backward_out(1, grad, done, 3, True)

                @pl.when(t >= 2)
                def _():
                    done = t - 2

                    def store(values):
                        gio_stage[lax.rem(done, 2)] = values

                        @pl.when(i == 0)
                        def _():
                            bufs[2, tile_rows(done), :] = values.astype(BF16)

                    backward_in(1, source, grad, done, 3, 2, True, store)

                    @pl.when(i == 0)
                    def _():
                        grad_pass(done).start()

                    gio_copy(i, done).start()
                    settle(lambda s: gio_copy(i, s), done, TILES)

        for t in range(TILES):
            grad_pass(t).wait_send()

    for part in range(5):
        for hop in range(1, 5):
            for way in range(2):
                ring_copy(part, hop, way).wait_send()
        share_copy(part, ring, 0, core).wait_send()
        for slot in range(1, 8):
            share_copy(part, ring, slot, core).wait_send()
    for half in range(2):
        cross_copy(half, section).wait_send()
    cross_params(section).wait_send()
    for t in range(TILES):
        raw_copy(t).wait_send()

    for target in (sibling, after, before):
        pl.semaphore_signal(ready, inc=1, device_id=target, device_id_type=MESH)
    pl.semaphore_wait(ready, 3)

    def grad_rows(pos):
        found = [(64 * pos, 64, 0), (D + 32 * pos, 32, 64), (D + H + 32 * pos, 32, 96)]
        for number, slot in enumerate((1, 2, 3, 0, 4)):
            found.append((2 * D + slot * H + 32 * pos, 32, 128 + 32 * number))
        return found

    def own_piece(pos):
        return jnp.concatenate(
            [acc[pl.ds(pl.multiple_of(first, 32), rows), :] for first, rows, _ in grad_rows(pos)], axis=0
        )

    sib_out = 0
    sib_land = RING * GRAD
    ring_land = 2 * RING * GRAD
    ring_stage = ring_land + 8 * GRAD

    def sib_copy(slot):
        src = weights.at[pl.ds(sib_out + slot * GRAD, GRAD)]
        dst = weights.at[pl.ds(sib_land + slot * GRAD, GRAD)]
        return remote(src, dst, red_send.at[2, slot], red_recv.at[2, slot], sibling)

    order = (4, 3, 5, 2, 6, 1, 7, 0)
    for slot in order:
        weights[pl.ds(sib_out + slot * GRAD, GRAD), :] = own_piece(position(ring + slot, 1 - core)).astype(BF16)
        sib_copy(slot).start()

    line = jnp.concatenate(
        [
            0.5 * jnp.sum(vec[0], axis=0, keepdims=True),
            0.5 * jnp.sum(vec[1, :, 0:D], axis=0, keepdims=True),
            jnp.sum(vec[2, :, 0:D], axis=0, keepdims=True),
            0.5 * jnp.sum(vec[1, :, D : 2 * D], axis=0, keepdims=True),
        ],
        axis=1,
    )
    for row in range(8):
        sums[0, row : row + 1, :] = line[:, row * 640 : (row + 1) * 640]

    def vec_share():
        return remote(sums.at[0], sums.at[1], vec_send.at[0], vec_recv.at[0], sibling)

    vec_share().start()

    def red_copy(way, step):
        rows = HALF if step == 1 else GRAD
        src = weights.at[pl.ds(ring_stage + (2 * way + step % 2) * GRAD, rows)]
        dst = weights.at[pl.ds(ring_land + (4 * way + step - 1) * GRAD, rows)]
        return remote(src, dst, red_send.at[way, step - 1], red_recv.at[way, step - 1], after if way == 0 else before)

    def both_cores(slot):
        pos = position(ring + slot, core)
        return own_piece(pos) + weights[pl.ds(sib_land + slot * GRAD, GRAD), :].astype(F32)

    def arrived(way, step):
        first = ring_land + (4 * way + step - 1) * GRAD
        if step == 1:
            half = weights[pl.ds(first, HALF), :].astype(F32)
            blank = jnp.zeros((HALF, H), F32)
            return jnp.concatenate([half, blank] if way == 0 else [blank, half], axis=0)
        return weights[pl.ds(first, GRAD), :].astype(F32)

    def vec_copy(way, hop):
        step = 1 if way == 0 else -1
        src = sums.at[2 + lax.rem(ring - step * (hop - 1) + 2 * RING, RING)]
        number = 1 + 4 * way + hop - 1
        return remote(src, src, vec_send.at[number], vec_recv.at[number], after if way == 0 else before)

    def vec_arrival(way, hop):
        step = 1 if way == 0 else -1
        dst = sums.at[2 + lax.rem(ring - step * hop + 2 * RING, RING)]
        number = 1 + 4 * way + hop - 1
        return remote(dst, dst, vec_send.at[number], vec_recv.at[number], after if way == 0 else before)

    sib_copy(4).wait_recv()
    farthest = both_cores(4).astype(BF16)
    for way in range(2):
        rows = pl.ds(ring_stage + (2 * way + 1) * GRAD, HALF)
        weights[rows, :] = farthest[0:HALF] if way == 0 else farthest[HALF:GRAD]
        red_copy(way, 1).start()
    vec_share().wait_recv()
    sums[2 + ring] = sums[0] + sums[1]
    for way in range(2):
        vec_copy(way, 1).start()
    for step in range(2, 5):
        for way in range(2):
            slot = 5 - step if way == 0 else 3 + step
            sib_copy(slot).wait_recv()
            red_copy(way, step - 1).wait_recv()
            total = both_cores(slot) + arrived(way, step - 1)
            if step > 2:
                red_copy(way, step - 2).wait_send()
            weights[pl.ds(ring_stage + (2 * way + step % 2) * GRAD, GRAD), :] = total.astype(BF16)
            red_copy(way, step).start()
        for way in range(2):
            vec_arrival(way, step - 1).wait_recv()
            if step < 4 or way == 0:
                vec_copy(way, step).start()
    sib_copy(0).wait_recv()
    total = both_cores(0)
    for way in range(2):
        red_copy(way, 4).wait_recv()
        total = total + arrived(way, 4)
    grad_in_out[...] = total[0:64]
    grad_out_out[0] = total[64:96]
    grad_out_out[1] = total[96:128]
    for slot in range(1, 4):
        grad_tap_out[slot] = total[96 + 32 * slot : 128 + 32 * slot]

    fifth = remote(tap_send, tap_land, tap_sem.at[0], tap_sem.at[1], peer)

    @pl.when(section == 0)
    def _():
        grad_tap_out[0] = total[224:256]
        tap_send[...] = total[256:288].astype(BF16)
        fifth.start()
        fifth.wait_send()

    vec_arrival(0, 4).wait_recv()
    line = sums[2]
    for chip_sum in range(1, RING):
        line = line + sums[2 + chip_sum]
    flat = jnp.concatenate([line[row : row + 1, :] for row in range(8)], axis=1)
    gain_out[...] = flat[:, 0 : 2 * D]
    bias_out[...] = flat[:, 2 * D : 5 * D]

    @pl.when(section == 1)
    def _():
        fifth.wait_recv()
        grad_tap_out[0] = tap_land[...].astype(F32)

    for way in range(2):
        for step in (3, 4):
            red_copy(way, step).wait_send()
        for hop in range(1, 5 if way == 0 else 4):
            vec_copy(way, hop).wait_send()
    for slot in range(RING):
        sib_copy(slot).wait_send()
    vec_share().wait_send()


def local(group, block_ends, proj_in, proj_out, conv_taps, norm_gains, bias_terms, lengths, dilation):
    micro, rows = block_ends.shape[1:3]
    if group > 1:
        proj_in = lax.all_gather(proj_in, "lane", axis=1, tiled=True)
        proj_out = lax.all_gather(proj_out, "lane", axis=1, tiled=True)
        conv_taps = lax.all_gather(conv_taps, "lane", axis=2, tiled=True)
    slots = conv_taps.reshape(4, 32, H)
    halves = proj_out.reshape(32, 2, H)
    piece = jnp.concatenate([slots[0], proj_in.reshape(64, H), halves[:, 0], halves[:, 1], slots[1], slots[2], slots[3]])
    params = jnp.concatenate([norm_gains, bias_terms], axis=1)
    vmem = pl.BlockSpec(memory_space=pltpu.VMEM)
    smem = pl.BlockSpec(memory_space=pltpu.SMEM)
    hbm = pl.BlockSpec(memory_space=pl.ANY)
    shape = jax.ShapeDtypeStruct
    dma = pltpu.SemaphoreType.DMA
    act, gio, grad_in, grad_out, grad_tap, gain_sum, bias_sum = pl.pallas_call(
        functools.partial(kernel, group),
        out_shape=[
            shape((micro, rows, D), BF16),
            shape((micro, rows, D), F32),
            shape((64, H), F32),
            shape((2, 32, H), F32),
            shape((4, 32, H), F32),
            shape((1, 2 * D), F32),
            shape((1, 3 * D), F32),
        ],
        in_specs=[smem, smem, hbm, vmem, vmem],
        out_specs=[hbm, hbm, vmem, vmem, vmem, vmem, vmem],
        scratch_shapes=[
            pltpu.VMEM((2 * POSITIONS * PIECE, H), BF16),
            pltpu.VMEM((micro, rows, D), BF16),
            pltpu.VMEM((3, LEN, D), BF16),
            pltpu.VMEM((5, PANELS, LEN + 2 * PAD, LANES), F32),
            pltpu.VMEM((LEN, D), BF16),
            pltpu.VMEM((LEN, H), BF16),
            pltpu.VMEM((LEN, H), BF16),
            pltpu.VMEM((2, 4, LEN, 1), F32),
            pltpu.VMEM((2, LEN, LANES), jnp.int32),
            pltpu.VMEM((ACC_ROWS, H), F32),
            pltpu.VMEM((3, 8, 2 * D), F32),
            pltpu.VMEM((2, TILE, D), F32),
            pltpu.VMEM((2, TILE, D), BF16),
            pltpu.VMEM((2, 1, STAT), F32),
            pltpu.VMEM((2 + RING, 8, 640), F32),
            pltpu.VMEM((32, H), BF16),
            pltpu.VMEM((32, H), BF16),
            dma((2, 5, 4)),
            dma((2, 5, 4)),
            dma((5, 8)),
            dma((5, 8)),
            dma((3,)),
            dma((3,)),
            dma((TILES,)),
            dma((TILES,)),
            dma((TILES,)),
            dma((TILES,)),
            dma((3,)),
            dma((2,)),
            dma((2,)),
            dma((3, 8)),
            dma((3, 8)),
            dma((9,)),
            dma((9,)),
            dma((2,)),
            pltpu.SemaphoreType.REGULAR,
        ],
        compiler_params=pltpu.CompilerParams(
            collective_id=0, has_side_effects=True, vmem_limit_bytes=64 << 20
        ),
        name="residual_blocks",
    )(dilation, lengths[:, 0, :], block_ends[0], piece, params)
    flat_out = jnp.stack([grad_out[0], grad_out[1]], axis=1)
    grads = (grad_in.reshape(1, -1), flat_out.reshape(1, -1), grad_tap.reshape(1, 4, -1))
    if group > 1:
        grads = tuple(
            lax.psum_scatter(part, "lane", scatter_dimension=part.ndim - 1, tiled=True) for part in grads
        )
        gain_sum, bias_sum = lax.psum((gain_sum, bias_sum), "lane")
    return (act[None], gio[None], *grads, gain_sum, bias_sum)


def solution(mesh):
    group = mesh.shape["dp"] // POSITIONS
    spread = "dp"
    if group > 1:
        mesh = Mesh(mesh.devices.reshape(2, POSITIONS, group), ("section", "dp", "lane"))
        spread = ("dp", "lane")
    placed = (
        P("section", None, spread, None),
        P("section", spread),
        P("section", spread),
        P("section", None, spread),
        P("section", None),
        P("section", None),
        P(None, spread, None),
        P(),
    )
    return jax.shard_map(
        functools.partial(local, group),
        mesh=mesh,
        in_specs=placed,
        out_specs=(
            P("section", None, spread, None),
            P("section", None, spread, None),
            P("section", spread),
            P("section", spread),
            P("section", None, spread),
            P("section", None),
            P("section", None),
        ),
        check_vma=False,
    )
```

time: 809 us -> 192 us (0.24)
  waiting for transfers between devices: 257 us -> 0 us
  other arithmetic: 224 us -> 3.88 us
  Pallas kernels: 0 us -> 165 us
  matrix products: 159 us -> 0 us
  blocking collectives: 60.5 us -> 0 us
  local copies, waits for them, and re-layouts: 69.4 us -> 22.7 us
  between operations: 18.6 us -> 0.73 us
  starting transfers between devices: 9.15 us -> 0 us
    pallas_call x0 -> x1, Pallas kernels: none -> 165 us  [local(): pl.pallas_call(functools.partial(kernel, group), out_shape=[shape((micro,...]
    dot_general x39 -> x0, matrix products: 143 us -> none  [the longest x15 56.2 us: product(): return jnp.dot(left, right, preferred_element_type=jnp.float32)]
    ppermute x6 -> x0, waiting for transfers between devices: 112 us -> none  [shifted(): lax.ppermute(value, axis, [(source, source + steps) for source in range(i...]
    unnamed x5 -> x0, waiting for transfers between devices: 85.6 us -> none
    mul x29 -> x0, other arithmetic: 67.1 us -> none  [the longest x23 56.1 us: tap_rows(): jnp.roll(shaped, -offset, axis=1) * tap_mask[:, :, None]]
    psum x1 -> x0, blocking collectives: 60.5 us -> none  [local(): gain_sum, bias_sum = lax.psum((gain_grads[None], bias_grads[None]), 'dp')]
    all_gather x3 -> x0, waiting for transfers between devices: 59.7 us -> none  [the longest x1 33.1 us: fetch(): lax.all_gather(proj_in, 'dp', axis=1, tiled=True)]
    reduce_sum x37 -> x0, other arithmetic: 51.2 us -> none  [the longest x7 24.2 us: norm_gelu(): return jax.nn.gelu(centre * lax.rsqrt(spread + epsilon) * gain + shift_bias)]
  transfers between devices with their start and end apart: 10 -> 0, of which waited for: 10 -> 0; matrix products, arithmetic and copies ran while one was open for 20% -> 0% of each run, Pallas kernels for 0% -> 0%
where the time goes in v1:
time: 192 us
  Pallas kernels  165 us (86%)
  local copies, waits for them, and re-layouts  22.7 us (12%)
  other arithmetic  3.88 us (2%)
    pallas_call x1, Pallas kernels, local(): pl.pallas_call(functools.partial(kernel, group), out_shape=[shape((micro,...  165 us
    unnamed x17, local copies, waits for them, and re-layouts  16.2 us

profile of v1, /device:TPU:0, one launch (start us, length us, event | category | flops | bytes accessed | tf_op | source)
XLA Modules:
  0.0 191.8 jit_solution(14929760210549068057)
XLA Ops:
  0.6 1.3 pad_maximum_fusion.1.params
  2.0 1.3 reduce.1
  3.2 0.1 reshape.38
  3.3 1.3 reduce.2
  4.6 0.1 fusion.2
  4.7 1.9 slice_reduce_fusion
  6.8 0.6 constant_dynamic-update-slice_fusion.4
  7.4 0.6 constant_dynamic-update-slice_fusion.3
  8.0 0.6 fusion.1
  8.6 0.6 fusion
  9.3 0.6 constant_dynamic-update-slice_fusion.2
  9.9 0.6 constant_dynamic-update-slice_fusion.1
  10.5 0.6 constant_dynamic-update-slice_fusion.piece
  11.1 164.5 %residual_blocks.1 = (bf16[2,1024,1024]{2,1,0:T(8,128)(2,1)}, f32[2,1024,1024]{2,1,0:T(8,128)}, f32[64,512]{1,0:T(8,128)}, f32[2,32,512]{2,1,0:T(8,128)}, f32[4,...) custom-call(s32[2]{0:T(128)} %dilation.1, s32[2,8]{1,0:T(2,128)} %bitcast.24, ...), custom_call_target="tpu_custom_call" | custom-call | tf_op jit(solution)/shard_map/residual_blocks/pallas_call | solution.py:772
  175.7 1.7 copy.20
  177.3 0.9 slice_bitcast_fusion.1
  178.2 0.1 copy.17
  178.4 0.9 reshape.41
  179.2 1.8 reshape.42
  181.0 0.0 copy-start
  181.0 4.9 %copy.37 = bf16[1,2,1024,1024]{3,2,1,0:T(8,128)(2,1)} copy(bf16[1,2,1024,1024]{3,2,1,0:T(8,128)(2,1)} %bitcast.21) | data formatting | bytes 8388608
  186.0 1.2 copy-done
  187.2 0.0 copy-start.2
  187.2 0.0 copy-start.1
  187.2 3.4 %copy.38 = f32[1,2,1024,1024]{3,2,1,0:T(8,128)} copy(f32[1,2,1024,1024]{3,2,1,0:T(8,128)S(1)} %bitcast.19) | data formatting | bytes 16777216
  190.6 0.0 copy-done.2
  190.6 0.6 copy.39
  191.2 0.0 copy-done.1
  191.2 0.6 copy.40
  (6 shorter events, 0.2 us)
Async XLA Ops:
  181.0 6.2 %copy-start = (f32[2,1024,1024]{2,1,0:T(8,128)S(1)}, f32[2,1024,1024]{2,1,0:T(8,128)}, u32[]{:S(2)}) copy-start(f32[2,1024,1024]{2,1,0:T(8,128)} %get-tuple-element.15) | copy-start | bytes 25165828
  187.2 3.4 %copy-start.2 = (f32[1,2048]{1,0:T(1,128)S(1)}, f32[1,2048]{1,0:T(1,128)}, u32[]{:S(2)}) copy-start(f32[1,2048]{1,0:T(1,128)} %get-tuple-element.41) | copy-start | bytes 24580
  187.2 4.0 %copy-start.1 = (f32[1,3072]{1,0:T(1,128)S(1)}, f32[1,3072]{1,0:T(1,128)}, u32[]{:S(2)}) copy-start(f32[1,3072]{1,0:T(1,128)} %get-tuple-element.42) | copy-start | bytes 36868
